TPU v7x, 32 devices: a whole 2x2x4 slice. The times are simulated.
32 devices in a mesh: phase: 4 (over y, x), tile: 4 (over z), dp: 2 (over core).
Axes of the slice: x: 2, y: 2, z: 4, core: 2. Of those that a mesh axis runs over, the one named last changes fastest.
Arguments:
- camera_feats: bfloat16 [4, 2, 3, 4, 176, 128], P(None, 'dp', None, 'tile'), may hold values from -6 to 6
- backbone_w: bfloat16 [4, 1152, 128], P('phase'), may hold values from -0.1875 to 0.1875
- depth_w: bfloat16 [128, 118], replicated, may hold values from -1 to 1
- block_tile: int32 [4, 2, 1056, 1], P('phase', 'dp', 'tile'), may hold values from 0 to 3; in each aligned block of 264 rows (0 to 263, 264 to 527, ..., all dimensions but the last counted through in order) at most 264 rows name the same one
- point_slot: int32 [4, 2, 1056, 236], P('phase', 'dp', 'tile'), may hold values from 0 to 15
- block_cells: int32 [4, 2, 1056, 16], P('phase', 'dp', 'tile'), may hold values from 0 to 1024, as said below
- bev_w: bfloat16 [1152, 128], replicated, may hold values from -0.1875 to 0.1875
- cotangent: bfloat16 [4, 2, 16, 256, 128], P('phase', 'dp', 'tile'), may hold values from -6 to 6
Outputs:
- encoded: bfloat16 [4, 2, 16, 256, 128], P('phase', 'dp', 'tile')
- conv_grad: float32 [128, 1152], P('tile')
Inputs may be any that keep to these rules, and one draw needn't show every extreme that they name: `block_tile`: among the 264 blocks of one sample on one index of tile (an aligned run of rows), at most 264 name the same tile. `block_cells`: 1024 marks a slot whose cell lies outside the grid.
All inputs are finite; a program needn't handle non-finite values.
Results may differ from a plain program's by a relative error of at most 0.0085.
Values may be sent and summed in bfloat16 or wider, within the bound.
A program may use at most 64 MiB of HBM per device.

v0:
```python
import jax
import jax.numpy as jnp
from jax import lax
from jax.sharding import PartitionSpec as P

NSEG = 2
BLK = 4


BOUND = 8.0


def extended(cells, sides, width):
    for axis, dim in sides:
        count = lax.axis_size(axis)
        ends = count - 1
        head = lax.slice_in_dim(cells, 0, width, axis=dim)
        tail = lax.slice_in_dim(cells, cells.shape[dim] - width, cells.shape[dim], axis=dim)
        cells = jnp.concatenate(
            [
                lax.ppermute(tail, axis, [(i, (i + 1) % count) for i in range(ends)]),
                cells,
                lax.ppermute(head, axis, [((i + 1) % count, i) for i in range(ends)]),
            ],
            axis=dim,
        )
    return cells


def passed_along(block, axis, distance):
    devices = range(lax.axis_size(axis))
    route = [(i - distance, i) for i in devices if i - distance in devices]
    return lax.ppermute(block, axis, route)


def from_root(block, axis, source):
    block = jnp.where(lax.axis_index(axis) == source, block, jnp.zeros_like(block))
    return lax.psum(block, axis)


def patches_from(padded, row_count, col_count):
    widened = jnp.pad(padded, [(0, 0)] * (padded.ndim - 2) + [(1, 1), (0, 0)])
    shifted = [
        widened[..., row_off : row_off + row_count, col_off : col_off + col_count, :]
        for row_off in range(3)
        for col_off in range(3)
    ]
    stacked = jnp.concatenate(shifted, axis=-1)
    return stacked.reshape(-1, stacked.shape[-1])


def section(images, weight):
    padded = extended(images, (("tile", 2),), 1)
    hidden = jnp.dot(
        patches_from(padded, images.shape[2], images.shape[3]),
        weight,
        preferred_element_type=jnp.float32,
    ).reshape(images.shape)
    return (images.astype(jnp.float32) + jax.nn.silu(hidden)).astype(jnp.bfloat16)


def body(camera_feats, backbone_w, depth_w, block_tile, point_slot, block_cells, bev_w, cotangent):
    phases = lax.axis_size("phase")
    phase_idx = lax.axis_index("phase")
    tile_count = lax.axis_size("tile")
    micro_all = camera_feats.shape[0]
    per_phase = micro_all // phases
    own_weight = backbone_w[0]
    carried = jnp.zeros_like(camera_feats[0])
    collected = jnp.zeros_like(camera_feats)
    steps_total = micro_all + phases - 1
    for step_idx in range(steps_total):
        if step_idx < micro_all:
            entering = jnp.where(phase_idx == 0, camera_feats[step_idx], carried)
        else:
            entering = carried
        leaving = section(entering, own_weight)
        finished = step_idx - (phases - 1)
        if finished >= 0:
            collected = collected.at[finished].set(
                jnp.where(phase_idx == phases - 1, leaving, collected[finished])
            )
        if step_idx + 1 < steps_total:
            carried = passed_along(leaving, "phase", 1)
    everything = from_root(collected, "phase", phases - 1)
    own_feats = lax.dynamic_slice_in_dim(everything, phase_idx * per_phase, per_phase, 0)
    samples_dev = own_feats.shape[0] * own_feats.shape[1]
    channels = own_feats.shape[-1]
    context = own_feats.reshape(samples_dev, -1, channels)
    positions = context.shape[1]
    seg_len = depth_w.shape[1] // NSEG
    slot_total = block_cells.shape[-1]
    pos_groups = positions // BLK
    block_count = pos_groups * NSEG
    logits = jnp.dot(context.reshape(-1, channels), depth_w, preferred_element_type=jnp.float32)
    depth_prob = jax.nn.softmax(BOUND * jnp.tanh(logits / BOUND), axis=-1)
    depth_blocks = (
        depth_prob.reshape(samples_dev, pos_groups, BLK, NSEG, seg_len)
        .transpose(0, 1, 3, 2, 4)
        .reshape(samples_dev, block_count, BLK, seg_len)
    )
    slot_blocks = point_slot.reshape(samples_dev, block_count, BLK, seg_len)
    splat_w = jnp.stack(
        [
            jnp.sum(
                jnp.where(slot_blocks == target, depth_blocks, jnp.zeros_like(depth_blocks)),
                axis=-1,
            )
            for target in range(slot_total)
        ],
        axis=2,
    ).astype(jnp.bfloat16)
    block_ctx = jnp.repeat(context.reshape(samples_dev, pos_groups, BLK, channels), NSEG, axis=1)
    row_count = cotangent.shape[2]
    col_count = cotangent.shape[3]
    cells_tile = row_count * col_count
    capacity = max(2, 4 * block_count // tile_count)
    targets = block_tile.reshape(samples_dev, block_count)
    member = (targets[..., None] == jnp.arange(tile_count, dtype=jnp.int32)).astype(jnp.int32)
    slot_rank = jnp.sum((jnp.cumsum(member, axis=1) - 1) * member, axis=-1)
    slot_flat = targets * capacity + slot_rank
    sample_rows = jnp.broadcast_to(
        jnp.arange(samples_dev, dtype=jnp.int32)[:, None], slot_flat.shape
    )
    send_ctx = (
        jnp.zeros((samples_dev, tile_count * capacity, BLK, channels), jnp.bfloat16)
        .at[sample_rows, slot_flat]
        .set(block_ctx)
    )
    send_weights = (
        jnp.zeros((samples_dev, tile_count * capacity, slot_total, BLK), jnp.bfloat16)
        .at[sample_rows, slot_flat]
        .set(splat_w)
    )
    send_cells = (
        jnp.full((samples_dev, tile_count * capacity, slot_total), cells_tile, jnp.int32)
        .at[sample_rows, slot_flat]
        .set(block_cells.reshape(samples_dev, block_count, slot_total))
    )
    send_ctx = send_ctx.reshape(samples_dev, tile_count, capacity, BLK, channels)
    send_weights = send_weights.reshape(samples_dev, tile_count, capacity, slot_total, BLK)
    send_cells = send_cells.reshape(samples_dev, tile_count, capacity, slot_total)
    got_ctx, got_weights, got_cells = (
        lax.all_to_all(send_ctx, "tile", split_axis=1, concat_axis=1, tiled=True),
        lax.all_to_all(send_weights, "tile", split_axis=1, concat_axis=1, tiled=True),
        lax.all_to_all(send_cells, "tile", split_axis=1, concat_axis=1, tiled=True),
    )
    pooled = jnp.einsum(
        "ankti,ankic->anktc", got_weights, got_ctx, preferred_element_type=jnp.float32
    ).astype(jnp.bfloat16)
    group_size = min(8, tile_count)
    group_count = tile_count // group_size
    group_rows = group_size * capacity * slot_total
    pooled_groups = jnp.moveaxis(
        pooled.reshape(samples_dev, group_count, group_rows, channels), 1, 0
    )
    cell_groups = jnp.moveaxis(got_cells.reshape(samples_dev, group_count, group_rows), 1, 0)
    cell_range = jnp.arange(cells_tile, dtype=jnp.int32).reshape(1, cells_tile, 1)

    def splat_group(grid_sum, pieces):
        part_pooled, part_cells = pieces
        one_hot = (part_cells[:, None, :] == cell_range).astype(jnp.bfloat16)
        grid_sum = grid_sum + jnp.einsum(
            "sxr,src->sxc", one_hot, part_pooled, preferred_element_type=jnp.float32
        )
        return (grid_sum, None)

    totals, _ = lax.scan(
        splat_group,
        jnp.zeros((samples_dev, cells_tile, channels), jnp.float32),
        (pooled_groups, cell_groups),
    )
    bev_grid = totals.astype(jnp.bfloat16).reshape(samples_dev, row_count, col_count, channels)
    padded_grid = extended(bev_grid, (("tile", 1),), 1)
    bev_patches = patches_from(padded_grid, row_count, col_count)
    mixed = jnp.dot(bev_patches, bev_w, preferred_element_type=jnp.float32)
    encoded = (
        (bev_grid.astype(jnp.float32).reshape(-1, channels) + mixed)
        .astype(jnp.bfloat16)
        .reshape(cotangent.shape)
    )
    upstream = cotangent.reshape(-1, channels)
    total_cells = (
        micro_all * cotangent.shape[1] * lax.axis_size("dp") * row_count * tile_count * col_count
    )
    grad_scale = float(total_cells) ** (-0.5)
    grad_share = lax.psum_scatter(
        grad_scale
        * lax.dot_general(
            upstream, bev_patches, (((0,), (0,)), ((), ())), preferred_element_type=jnp.float32
        ),
        "tile",
        scatter_dimension=0,
        tiled=True,
    )
    conv_grad = lax.psum(grad_share, ("phase", "dp"))
    return (encoded, conv_grad)


def solution(mesh):
    return jax.shard_map(
        body,
        mesh=mesh,
        in_specs=(
            P(None, "dp", None, "tile", None, None),
            P("phase", None, None),
            P(),
            P("phase", "dp", "tile", None),
            P("phase", "dp", "tile", None),
            P("phase", "dp", "tile", None),
            P(),
            P("phase", "dp", "tile", None, None),
        ),
        out_specs=(P("phase", "dp", "tile", None, None), P("tile", None)),
        check_vma=False,
    )
```

profile of v0, /device:TPU:0, one launch (start us, length us, event | category | flops | bytes accessed | tf_op | source)
XLA Modules:
  0.0 385.1 jit_solution(11881665665288128379)
XLA Ops:
  8.2 4.9 %collective-permute-start = (bf16[1,3,1,176,128]{4,3,1,2,0:T(8,128)(2,1)S(1)}, bf16[1,3,1,176,128]{4,3,1,2,0:T(8,128)(2,1)S(1)}, u32[]{:S(2)}, u32[]{:S(2)}) collective-permute-start(bf16[1,3,1,176,128]{4,3,1,2,0:T(8,128)(2,1)S(1)} %fusion.83), channel_id=1, source_target_pairs={{0,2},{2,4},{4,6},{1,3},{3,5},{5,7},{8,10},{10,12},{12,14},{9,11},... | collective-permute-start | bytes 405512 | tf_op jit(solution)/shard_map/ppermute | solution.py:21
  15.9 4.1 %collective-permute-done.1 = bf16[1,3,1,176,128]{4,3,1,2,0:T(8,128)(2,1)S(1)} collective-permute-done((bf16[1,3,1,176,128]{4,3,1,2,0:T(8,128)(2,1)S(1)}, bf16[1,3,1,176,128]{4,3,1,2,0:T(8,128)(2,1)S(1)}, u32[]{:S(2)}, u32[]{:S(2)}) %collective-permute-start.1) | collective-permute-done | bytes 135200 | tf_op jit(solution)/shard_map/ppermute | solution.py:23
  21.8 3.4 collective-permute-start.2
  25.2 2.5 collective-permute-done.2
  27.8 3.5 collective-permute-start.3
  33.8 4.4 %collective-permute-done.4 = bf16[1,3,1,176,128]{4,3,1,2,0:T(8,128)(2,1)S(1)} collective-permute-done((bf16[1,3,1,176,128]{4,3,1,2,0:T(8,128)(2,1)S(1)}, bf16[1,3,1,176,128]{4,3,1,2,0:T(8,128)(2,1)S(1)}, u32[]{:S(2)}, u32[]{:S(2)}) %collective-permute-start.4) | collective-permute-done | bytes 135200 | tf_op jit(solution)/shard_map/ppermute | solution.py:23
  39.3 4.4 %collective-permute-start.5 = (bf16[1,3,1,176,128]{4,3,1,2,0:T(8,128)(2,1)S(1)}, bf16[1,3,1,176,128]{4,3,1,2,0:T(8,128)(2,1)S(1)}, u32[]{:S(2)}, u32[]{:S(2)}) collective-permute-start(bf16[1,3,1,176,128]{4,3,1,2,0:T(8,128)(2,1)S(1)} %add_convert_fusion.5), channel_id=1, source_target_pairs={{0,8},{8,16},{16,24},{1,9},{9,17},{17,25},{2,10},{10,18},{18,26},{... | collective-permute-start | bytes 405512 | tf_op jit(solution)/shard_map/ppermute | solution.py:33
  43.7 2.5 collective-permute-done.5
  46.3 3.5 collective-permute-start.6
  52.3 4.4 %collective-permute-done.7 = bf16[1,3,1,176,128]{4,3,1,2,0:T(8,128)(2,1)S(1)} collective-permute-done((bf16[1,3,1,176,128]{4,3,1,2,0:T(8,128)(2,1)S(1)}, bf16[1,3,1,176,128]{4,3,1,2,0:T(8,128)(2,1)S(1)}, u32[]{:S(2)}, u32[]{:S(2)}) %collective-permute-start.7) | collective-permute-done | bytes 135200 | tf_op jit(solution)/shard_map/ppermute | solution.py:23
  57.8 4.4 %collective-permute-start.8 = (bf16[1,3,1,176,128]{4,3,1,2,0:T(8,128)(2,1)S(1)}, bf16[1,3,1,176,128]{4,3,1,2,0:T(8,128)(2,1)S(1)}, u32[]{:S(2)}, u32[]{:S(2)}) collective-permute-start(bf16[1,3,1,176,128]{4,3,1,2,0:T(8,128)(2,1)S(1)} %add_convert_fusion.4), channel_id=1, source_target_pairs={{0,8},{8,16},{16,24},{1,9},{9,17},{17,25},{2,10},{10,18},{18,26},{... | collective-permute-start | bytes 405512 | tf_op jit(solution)/shard_map/ppermute | solution.py:33
  66.1 4.6 %collective-permute-start.9 = (bf16[1,3,1,176,128]{4,3,1,2,0:T(8,128)(2,1)S(1)}, bf16[1,3,1,176,128]{4,3,1,2,0:T(8,128)(2,1)S(1)}, u32[]{:S(2)}, u32[]{:S(2)}) collective-permute-start(bf16[1,3,1,176,128]{4,3,1,2,0:T(8,128)(2,1)S(1)} %fusion.57), channel_id=1, source_target_pairs={{0,2},{2,4},{4,6},{1,3},{3,5},{5,7},{8,10},{10,12},{12,14},{9,11},... | collective-permute-start | bytes 405512 | tf_op jit(solution)/shard_map/ppermute | solution.py:21
  74.4 5.2 %collective-permute-start.11 = (bf16[1,3,1,176,128]{4,3,1,2,0:T(8,128)(2,1)S(1)}, bf16[1,3,1,176,128]{4,3,1,2,0:T(8,128)(2,1)S(1)}, u32[]{:S(2)}, u32[]{:S(2)}) collective-permute-start(bf16[1,3,1,176,128]{4,3,1,2,0:T(8,128)(2,1)S(1)} %get-tuple-element.92), channel_id=1, source_target_pairs={{0,8},{8,16},{16,24},{1,9},{9,17},{17,25},{2,10},{10,18},{18,26},{... | collective-permute-start | bytes 405512 | tf_op jit(solution)/shard_map/ppermute | solution.py:33
  79.6 2.5 collective-permute-done.11
  82.1 4.4 %collective-permute-start.12 = (bf16[1,3,1,176,128]{4,3,1,2,0:T(8,128)(2,1)S(1)}, bf16[1,3,1,176,128]{4,3,1,2,0:T(8,128)(2,1)S(1)}, u32[]{:S(2)}, u32[]{:S(2)}) collective-permute-start(bf16[1,3,1,176,128]{4,3,1,2,0:T(8,128)(2,1)S(1)} %collective-permute-done.11), channel_id=1, source_target_pairs={{0,2},{2,4},{4,6},{1,3},{3,5},{5,7},{8,10},{10,12},{12,14},{9,11},... | collective-permute-start | bytes 405512 | tf_op jit(solution)/shard_map/ppermute | solution.py:21
  89.0 4.4 %collective-permute-done.13 = bf16[1,3,1,176,128]{4,3,1,2,0:T(8,128)(2,1)S(1)} collective-permute-done((bf16[1,3,1,176,128]{4,3,1,2,0:T(8,128)(2,1)S(1)}, bf16[1,3,1,176,128]{4,3,1,2,0:T(8,128)(2,1)S(1)}, u32[]{:S(2)}, u32[]{:S(2)}) %collective-permute-start.13) | collective-permute-done | bytes 135200 | tf_op jit(solution)/shard_map/ppermute | solution.py:23
  94.6 5.3 %collective-permute-start.14 = (bf16[1,3,1,176,128]{4,3,1,2,0:T(8,128)(2,1)S(1)}, bf16[1,3,1,176,128]{4,3,1,2,0:T(8,128)(2,1)S(1)}, u32[]{:S(2)}, u32[]{:S(2)}) collective-permute-start(bf16[1,3,1,176,128]{4,3,1,2,0:T(8,128)(2,1)S(1)} %get-tuple-element.90), channel_id=1, source_target_pairs={{0,8},{8,16},{16,24},{1,9},{9,17},{17,25},{2,10},{10,18},{18,26},{... | collective-permute-start | bytes 405512 | tf_op jit(solution)/shard_map/ppermute | solution.py:33
  107.1 4.1 %collective-permute-done.16 = bf16[1,3,1,176,128]{4,3,1,2,0:T(8,128)(2,1)S(1)} collective-permute-done((bf16[1,3,1,176,128]{4,3,1,2,0:T(8,128)(2,1)S(1)}, bf16[1,3,1,176,128]{4,3,1,2,0:T(8,128)(2,1)S(1)}, u32[]{:S(2)}, u32[]{:S(2)}) %collective-permute-start.16) | collective-permute-done | bytes 135200 | tf_op jit(solution)/shard_map/ppermute | solution.py:23
  112.4 5.3 %collective-permute-start.17 = (bf16[1,3,1,176,128]{4,3,1,2,0:T(8,128)(2,1)S(1)}, bf16[1,3,1,176,128]{4,3,1,2,0:T(8,128)(2,1)S(1)}, u32[]{:S(2)}, u32[]{:S(2)}) collective-permute-start(bf16[1,3,1,176,128]{4,3,1,2,0:T(8,128)(2,1)S(1)} %get-tuple-element.88), channel_id=1, source_target_pairs={{0,8},{8,16},{16,24},{1,9},{9,17},{17,25},{2,10},{10,18},{18,26},{... | collective-permute-start | bytes 405512 | tf_op jit(solution)/shard_map/ppermute | solution.py:33
  124.7 4.4 %collective-permute-done.19 = bf16[1,3,1,176,128]{4,3,1,2,0:T(8,128)(2,1)S(1)} collective-permute-done((bf16[1,3,1,176,128]{4,3,1,2,0:T(8,128)(2,1)S(1)}, bf16[1,3,1,176,128]{4,3,1,2,0:T(8,128)(2,1)S(1)}, u32[]{:S(2)}, u32[]{:S(2)}) %collective-permute-start.19) | collective-permute-done | bytes 135200 | tf_op jit(solution)/shard_map/ppermute | solution.py:23
  133.5 3.5 all-to-all-start
  141.2 36.8 %all-reduce.14.cloned.1.call-done = bf16[4,1,3,1,176,128]{5,4,2,3,1,0:T(8,128)(2,1)} async-done(((bf16[4,1,3,1,176,128]{5,4,2,3,1,0:T(8,128)(2,1)}), bf16[4,1,3,1,176,128]{5,4,2,3,1,0:T(8,128)(2,1)}) %all-reduce.14.cloned.1.call-update) | async-done | bytes 540688 | tf_op jit(solution)/shard_map/psum | solution.py:38
  180.1 7.7 %fusion.26 = (bf16[132,2,4]{2,1,0:T(2,128)(2,1)S(1)}, bf16[132,2,4]{2,1,0:T(2,128)(2,1)S(1)}, bf16[132,2,4]{2,1,0:T(2,128)(2,1)S(1)}, bf16[132,2,4]{2,1,0:T(2,12...) fusion(pred[1,132,2,4,59]{4,3,2,1,0:T(4,128)(4,1)S(1)} %eq.411,, ...), kind=kLoop, calls=%fused_computation.54 | loop fusion | flops 1976832 | bytes 1279872 | tf_op jit(solution)/shard_map/reduce_sum | solution.py:105
  202.1 8.6 %scatter_fusion = bf16[1056,16,4]{1,2,0:T(4,128)(2,1)S(1)} fusion(bf16[1056,16,4]{1,2,0:T(4,128)(2,1)S(1)} %broadcast.618, s32[264]{0:T(512)S(1)} %fusion.62, bf16[264,16,4]{1,2,0:T(4,128)(2,1)S(1)} %copy.70), kind=kCustom, calls=%fused_computation.1 | custom fusion | bytes 102432 | tf_op jit(solution)/shard_map/scatter | solution.py:133
  212.0 4.6 %all-to-all-start.1 = ((bf16[1,4,264,16,4]{2,3,4,0,1:T(8,128)(2,1)}), bf16[1,4,264,16,4]{2,3,4,0,1:T(8,128)(2,1)S(1)}, u32[]{:S(2)}, u32[]{:S(2)}) async-start(bf16[1,4,264,16,4]{2,3,4,0,1:T(8,128)(2,1)} %copy.71), calls=%async_computation.1 | async-start | bytes 393216 | tf_op jit(solution)/shard_map/all_to_all | solution.py:145
  217.8 26.6 %scatter_fusion.1 = bf16[1056,4,128]{2,1,0:T(4,128)(2,1)} fusion(bf16[1056,4,128]{2,1,0:T(4,128)(2,1)} %broadcast.620, s32[264]{0:T(512)S(1)} %fusion.62, bf16[264,4,128]{2,1,0:T(4,128)(2,1)S(1)} %bitcast.272), kind=kCustom, calls=%fused_computation.2 | custom fusion | bytes 812064 | tf_op jit(solution)/shard_map/scatter | solution.py:128
  244.4 5.2 %all-to-all-start.2 = ((bf16[1,4,264,4,128]{4,3,2,0,1:T(4,128)(2,1)}), bf16[1,4,264,4,128]{4,3,2,0,1:T(4,128)(2,1)S(1)}, u32[]{:S(2)}, u32[]{:S(2)}) async-start(bf16[1,4,264,4,128]{4,3,2,0,1:T(4,128)(2,1)} %bitcast.70), calls=%async_computation.2 | async-start | bytes 2162688 | tf_op jit(solution)/shard_map/all_to_all | solution.py:144
  250.7 24.5 %all-to-all-done.2 = bf16[1,4,264,4,128]{4,3,2,0,1:T(4,128)(2,1)S(1)} async-done(((bf16[1,4,264,4,128]{4,3,2,0,1:T(4,128)(2,1)}), bf16[1,4,264,4,128]{4,3,2,0,1:T(4,128)(2,1)S(1)}, u32[]{:S(2)}, u32[]{:S(2)}) %all-to-all-start.2) | async-done | bytes 1081376 | tf_op jit(solution)/shard_map/all_to_all | solution.py:144
  277.0 10.5 %fusion.4 = bf16[1024,128]{1,0:T(8,128)(2,1)S(1)} fusion(bf16[16896,128]{1,0:T(8,128)(2,1)S(1)} %bitcast.247, s32[16896]{0:T(1024)S(1)} %eq.358), kind=kOutput, calls=%fused_computation.15 | convolution fusion | flops 4446617600 | bytes 4655104 | tf_op jit(solution)/shard_map/while/body/eval_jaxpr/sxr,src->sxc/dot_general | solution.py:163
  290.7 4.3 %collective-permute-done.21 = bf16[1,1,256,128]{3,2,1,0:T(8,128)(2,1)S(1)} collective-permute-done((bf16[1,1,256,128]{3,2,1,0:T(8,128)(2,1)S(1)}, bf16[1,1,256,128]{3,2,1,0:T(8,128)(2,1)S(1)}, u32[]{:S(2)}, u32[]{:S(2)}) %collective-permute-start.21) | collective-permute-done | bytes 65568 | tf_op jit(solution)/shard_map/ppermute | solution.py:23
  298.6 21.6 %reduce-scatter.4.cloned.1.call-done = f32[32,1152]{1,0:T(8,128)} async-done(((f32[128,1152]{1,0:T(8,128)}), f32[32,1152]{1,0:T(8,128)}) %reduce-scatter.4.cloned.1.call-update) | async-done | bytes 147472
  323.7 52.9 %all-reduce.16.cloned.1.call-done = f32[32,1152]{0,1:T(8,128)} async-done(((f32[32,1152]{0,1:T(8,128)}), f32[32,1152]{0,1:T(8,128)}) %all-reduce.16.cloned.1.call-update) | async-done | bytes 147472 | tf_op jit(solution)/shard_map/psum | solution.py:196
  (224 shorter events, 81.3 us)
Async XLA Ops:
  7.2 13.6 %copy-start = (bf16[1,1152,128]{2,1,0:T(8,128)(2,1)S(1)}, bf16[1,1152,128]{2,1,0:T(8,128)(2,1)}, u32[]{:S(2)}) copy-start(bf16[1,1152,128]{2,1,0:T(8,128)(2,1)} %param.17) | copy-start | bytes 884740
  7.2 170.8 %all-reduce.14.cloned.1.call-start = ((), (), s32[]{:S(2)}) async-start(), calls=%async_computation.4 | async-start | bytes 1081344 | tf_op jit(solution)/shard_map/psum | solution.py:38
  8.2 7.8 %collective-permute-start = (bf16[1,3,1,176,128]{4,3,1,2,0:T(8,128)(2,1)S(1)}, bf16[1,3,1,176,128]{4,3,1,2,0:T(8,128)(2,1)S(1)}, u32[]{:S(2)}, u32[]{:S(2)}) collective-permute-start(bf16[1,3,1,176,128]{4,3,1,2,0:T(8,128)(2,1)S(1)} %fusion.83), channel_id=1, source_target_pairs={{0,2},{2,4},{4,6},{1,3},{3,5},{5,7},{8,10},{10,12},{12,14},{9,11},... | collective-permute-start | bytes 405512 | tf_op jit(solution)/shard_map/ppermute | solution.py:21
  13.1 6.9 %collective-permute-start.1 = (bf16[1,3,1,176,128]{4,3,1,2,0:T(8,128)(2,1)S(1)}, bf16[1,3,1,176,128]{4,3,1,2,0:T(8,128)(2,1)S(1)}, u32[]{:S(2)}, u32[]{:S(2)}) collective-permute-start(bf16[1,3,1,176,128]{4,3,1,2,0:T(8,128)(2,1)S(1)} %fusion.83), channel_id=1, source_target_pairs={{2,0},{4,2},{6,4},{3,1},{5,3},{7,5},{10,8},{12,10},{14,12},{11,9},... | collective-permute-start | bytes 405512 | tf_op jit(solution)/shard_map/ppermute | solution.py:23
  21.8 5.9 %collective-permute-start.2 = (bf16[1,3,1,176,128]{4,3,1,2,0:T(8,128)(2,1)S(1)}, bf16[1,3,1,176,128]{4,3,1,2,0:T(8,128)(2,1)S(1)}, u32[]{:S(2)}, u32[]{:S(2)}) collective-permute-start(bf16[1,3,1,176,128]{4,3,1,2,0:T(8,128)(2,1)S(1)} %add_convert_fusion.6), channel_id=1, source_target_pairs={{0,8},{8,16},{16,24},{1,9},{9,17},{17,25},{2,10},{10,18},{18,26},{... | collective-permute-start | bytes 405512 | tf_op jit(solution)/shard_map/ppermute | solution.py:33
  27.8 6.0 %collective-permute-start.3 = (bf16[1,3,1,176,128]{4,3,1,2,0:T(8,128)(2,1)S(1)}, bf16[1,3,1,176,128]{4,3,1,2,0:T(8,128)(2,1)S(1)}, u32[]{:S(2)}, u32[]{:S(2)}) collective-permute-start(bf16[1,3,1,176,128]{4,3,1,2,0:T(8,128)(2,1)S(1)} %fusion.56), channel_id=1, source_target_pairs={{0,2},{2,4},{4,6},{1,3},{3,5},{5,7},{8,10},{10,12},{12,14},{9,11},... | collective-permute-start | bytes 405512 | tf_op jit(solution)/shard_map/ppermute | solution.py:21
  31.3 6.9 %collective-permute-start.4 = (bf16[1,3,1,176,128]{4,3,1,2,0:T(8,128)(2,1)S(1)}, bf16[1,3,1,176,128]{4,3,1,2,0:T(8,128)(2,1)S(1)}, u32[]{:S(2)}, u32[]{:S(2)}) collective-permute-start(bf16[1,3,1,176,128]{4,3,1,2,0:T(8,128)(2,1)S(1)} %fusion.56), channel_id=1, source_target_pairs={{2,0},{4,2},{6,4},{3,1},{5,3},{7,5},{10,8},{12,10},{14,12},{11,9},... | collective-permute-start | bytes 405512 | tf_op jit(solution)/shard_map/ppermute | solution.py:23
  39.3 6.9 %collective-permute-start.5 = (bf16[1,3,1,176,128]{4,3,1,2,0:T(8,128)(2,1)S(1)}, bf16[1,3,1,176,128]{4,3,1,2,0:T(8,128)(2,1)S(1)}, u32[]{:S(2)}, u32[]{:S(2)}) collective-permute-start(bf16[1,3,1,176,128]{4,3,1,2,0:T(8,128)(2,1)S(1)} %add_convert_fusion.5), channel_id=1, source_target_pairs={{0,8},{8,16},{16,24},{1,9},{9,17},{17,25},{2,10},{10,18},{18,26},{... | collective-permute-start | bytes 405512 | tf_op jit(solution)/shard_map/ppermute | solution.py:33
  46.3 6.0 %collective-permute-start.6 = (bf16[1,3,1,176,128]{4,3,1,2,0:T(8,128)(2,1)S(1)}, bf16[1,3,1,176,128]{4,3,1,2,0:T(8,128)(2,1)S(1)}, u32[]{:S(2)}, u32[]{:S(2)}) collective-permute-start(bf16[1,3,1,176,128]{4,3,1,2,0:T(8,128)(2,1)S(1)} %bitcast_select_fusion.16), channel_id=1, source_target_pairs={{0,2},{2,4},{4,6},{1,3},{3,5},{5,7},{8,10},{10,12},{12,14},{9,11},... | collective-permute-start | bytes 405512 | tf_op jit(solution)/shard_map/ppermute | solution.py:21
  49.8 6.9 %collective-permute-start.7 = (bf16[1,3,1,176,128]{4,3,1,2,0:T(8,128)(2,1)S(1)}, bf16[1,3,1,176,128]{4,3,1,2,0:T(8,128)(2,1)S(1)}, u32[]{:S(2)}, u32[]{:S(2)}) collective-permute-start(bf16[1,3,1,176,128]{4,3,1,2,0:T(8,128)(2,1)S(1)} %bitcast_select_fusion.16), channel_id=1, source_target_pairs={{2,0},{4,2},{6,4},{3,1},{5,3},{7,5},{10,8},{12,10},{14,12},{11,9},... | collective-permute-start | bytes 405512 | tf_op jit(solution)/shard_map/ppermute | solution.py:23
  57.8 6.9 %collective-permute-start.8 = (bf16[1,3,1,176,128]{4,3,1,2,0:T(8,128)(2,1)S(1)}, bf16[1,3,1,176,128]{4,3,1,2,0:T(8,128)(2,1)S(1)}, u32[]{:S(2)}, u32[]{:S(2)}) collective-permute-start(bf16[1,3,1,176,128]{4,3,1,2,0:T(8,128)(2,1)S(1)} %add_convert_fusion.4), channel_id=1, source_target_pairs={{0,8},{8,16},{16,24},{1,9},{9,17},{17,25},{2,10},{10,18},{18,26},{... | collective-permute-start | bytes 405512 | tf_op jit(solution)/shard_map/ppermute | solution.py:33
  64.8 6.9 %collective-permute-start.10 = (bf16[1,3,1,176,128]{4,3,1,2,0:T(8,128)(2,1)S(1)}, bf16[1,3,1,176,128]{4,3,1,2,0:T(8,128)(2,1)S(1)}, u32[]{:S(2)}, u32[]{:S(2)}) collective-permute-start(bf16[1,3,1,176,128]{4,3,1,2,0:T(8,128)(2,1)S(1)} %fusion.57), channel_id=1, source_target_pairs={{2,0},{4,2},{6,4},{3,1},{5,3},{7,5},{10,8},{12,10},{14,12},{11,9},... | collective-permute-start | bytes 405512 | tf_op jit(solution)/shard_map/ppermute | solution.py:23
  66.1 7.1 %collective-permute-start.9 = (bf16[1,3,1,176,128]{4,3,1,2,0:T(8,128)(2,1)S(1)}, bf16[1,3,1,176,128]{4,3,1,2,0:T(8,128)(2,1)S(1)}, u32[]{:S(2)}, u32[]{:S(2)}) collective-permute-start(bf16[1,3,1,176,128]{4,3,1,2,0:T(8,128)(2,1)S(1)} %fusion.57), channel_id=1, source_target_pairs={{0,2},{2,4},{4,6},{1,3},{3,5},{5,7},{8,10},{10,12},{12,14},{9,11},... | collective-permute-start | bytes 405512 | tf_op jit(solution)/shard_map/ppermute | solution.py:21
  74.4 7.7 %collective-permute-start.11 = (bf16[1,3,1,176,128]{4,3,1,2,0:T(8,128)(2,1)S(1)}, bf16[1,3,1,176,128]{4,3,1,2,0:T(8,128)(2,1)S(1)}, u32[]{:S(2)}, u32[]{:S(2)}) collective-permute-start(bf16[1,3,1,176,128]{4,3,1,2,0:T(8,128)(2,1)S(1)} %get-tuple-element.92), channel_id=1, source_target_pairs={{0,8},{8,16},{16,24},{1,9},{9,17},{17,25},{2,10},{10,18},{18,26},{... | collective-permute-start | bytes 405512 | tf_op jit(solution)/shard_map/ppermute | solution.py:33
  82.1 6.9 %collective-permute-start.12 = (bf16[1,3,1,176,128]{4,3,1,2,0:T(8,128)(2,1)S(1)}, bf16[1,3,1,176,128]{4,3,1,2,0:T(8,128)(2,1)S(1)}, u32[]{:S(2)}, u32[]{:S(2)}) collective-permute-start(bf16[1,3,1,176,128]{4,3,1,2,0:T(8,128)(2,1)S(1)} %collective-permute-done.11), channel_id=1, source_target_pairs={{0,2},{2,4},{4,6},{1,3},{3,5},{5,7},{8,10},{10,12},{12,14},{9,11},... | collective-permute-start | bytes 405512 | tf_op jit(solution)/shard_map/ppermute | solution.py:21
  86.5 6.9 %collective-permute-start.13 = (bf16[1,3,1,176,128]{4,3,1,2,0:T(8,128)(2,1)S(1)}, bf16[1,3,1,176,128]{4,3,1,2,0:T(8,128)(2,1)S(1)}, u32[]{:S(2)}, u32[]{:S(2)}) collective-permute-start(bf16[1,3,1,176,128]{4,3,1,2,0:T(8,128)(2,1)S(1)} %collective-permute-done.11), channel_id=1, source_target_pairs={{2,0},{4,2},{6,4},{3,1},{5,3},{7,5},{10,8},{12,10},{14,12},{11,9},... | collective-permute-start | bytes 405512 | tf_op jit(solution)/shard_map/ppermute | solution.py:23
  93.9 5.9 %copy-start.6 = (s32[1,1,264,1]{2,3,1,0:T(1,128)S(1)}, s32[1,1,264,1]{2,3,1,0:T(1,128)}, u32[]{:S(2)}) copy-start(s32[1,1,264,1]{2,3,1,0:T(1,128)} %param.19) | copy-start | bytes 3172
  94.6 7.8 %collective-permute-start.14 = (bf16[1,3,1,176,128]{4,3,1,2,0:T(8,128)(2,1)S(1)}, bf16[1,3,1,176,128]{4,3,1,2,0:T(8,128)(2,1)S(1)}, u32[]{:S(2)}, u32[]{:S(2)}) collective-permute-start(bf16[1,3,1,176,128]{4,3,1,2,0:T(8,128)(2,1)S(1)} %get-tuple-element.90), channel_id=1, source_target_pairs={{0,8},{8,16},{16,24},{1,9},{9,17},{17,25},{2,10},{10,18},{18,26},{... | collective-permute-start | bytes 405512 | tf_op jit(solution)/shard_map/ppermute | solution.py:33
  102.4 4.7 %collective-permute-start.15 = (bf16[1,3,1,176,128]{4,3,1,2,0:T(8,128)(2,1)S(1)}, bf16[1,3,1,176,128]{4,3,1,2,0:T(8,128)(2,1)S(1)}, u32[]{:S(2)}, u32[]{:S(2)}) collective-permute-start(bf16[1,3,1,176,128]{4,3,1,2,0:T(8,128)(2,1)S(1)} %collective-permute-done.14), channel_id=1, source_target_pairs={{0,2},{2,4},{4,6},{1,3},{3,5},{5,7},{8,10},{10,12},{12,14},{9,11},... | collective-permute-start | bytes 405512 | tf_op jit(solution)/shard_map/ppermute | solution.py:21
  104.3 6.9 %collective-permute-start.16 = (bf16[1,3,1,176,128]{4,3,1,2,0:T(8,128)(2,1)S(1)}, bf16[1,3,1,176,128]{4,3,1,2,0:T(8,128)(2,1)S(1)}, u32[]{:S(2)}, u32[]{:S(2)}) collective-permute-start(bf16[1,3,1,176,128]{4,3,1,2,0:T(8,128)(2,1)S(1)} %collective-permute-done.14), channel_id=1, source_target_pairs={{2,0},{4,2},{6,4},{3,1},{5,3},{7,5},{10,8},{12,10},{14,12},{11,9},... | collective-permute-start | bytes 405512 | tf_op jit(solution)/shard_map/ppermute | solution.py:23
  112.4 7.8 %collective-permute-start.17 = (bf16[1,3,1,176,128]{4,3,1,2,0:T(8,128)(2,1)S(1)}, bf16[1,3,1,176,128]{4,3,1,2,0:T(8,128)(2,1)S(1)}, u32[]{:S(2)}, u32[]{:S(2)}) collective-permute-start(bf16[1,3,1,176,128]{4,3,1,2,0:T(8,128)(2,1)S(1)} %get-tuple-element.88), channel_id=1, source_target_pairs={{0,8},{8,16},{16,24},{1,9},{9,17},{17,25},{2,10},{10,18},{18,26},{... | collective-permute-start | bytes 405512 | tf_op jit(solution)/shard_map/ppermute | solution.py:33
  120.2 4.4 %collective-permute-start.18 = (bf16[1,3,1,176,128]{4,3,1,2,0:T(8,128)(2,1)S(1)}, bf16[1,3,1,176,128]{4,3,1,2,0:T(8,128)(2,1)S(1)}, u32[]{:S(2)}, u32[]{:S(2)}) collective-permute-start(bf16[1,3,1,176,128]{4,3,1,2,0:T(8,128)(2,1)S(1)} %collective-permute-done.17), channel_id=1, source_target_pairs={{0,2},{2,4},{4,6},{1,3},{3,5},{5,7},{8,10},{10,12},{12,14},{9,11},... | collective-permute-start | bytes 405512 | tf_op jit(solution)/shard_map/ppermute | solution.py:21
  122.2 6.9 %collective-permute-start.19 = (bf16[1,3,1,176,128]{4,3,1,2,0:T(8,128)(2,1)S(1)}, bf16[1,3,1,176,128]{4,3,1,2,0:T(8,128)(2,1)S(1)}, u32[]{:S(2)}, u32[]{:S(2)}) collective-permute-start(bf16[1,3,1,176,128]{4,3,1,2,0:T(8,128)(2,1)S(1)} %collective-permute-done.17), channel_id=1, source_target_pairs={{2,0},{4,2},{6,4},{3,1},{5,3},{7,5},{10,8},{12,10},{14,12},{11,9},... | collective-permute-start | bytes 405512 | tf_op jit(solution)/shard_map/ppermute | solution.py:23
  133.5 78.5 %all-to-all-start = ((s32[1,4,264,16]{2,3,0,1:T(8,128)}), s32[1,4,264,16]{2,3,0,1:T(8,128)S(1)}, u32[]{:S(2)}, u32[]{:S(2)}) async-start(s32[1,4,264,16]{2,3,0,1:T(8,128)} %copy.48), calls=%async_computation | async-start | bytes 196608 | tf_op jit(solution)/shard_map/all_to_all | solution.py:146
  138.7 40.2 %copy-start.4 = (bf16[128,118]{0,1:T(8,128)(2,1)S(1)}, bf16[128,118]{0,1:T(8,128)(2,1)}, u32[]{:S(2)}) copy-start(bf16[128,118]{0,1:T(8,128)(2,1)} %param.18) | copy-start | bytes 90628
  212.0 32.4 %all-to-all-start.1 = ((bf16[1,4,264,16,4]{2,3,4,0,1:T(8,128)(2,1)}), bf16[1,4,264,16,4]{2,3,4,0,1:T(8,128)(2,1)S(1)}, u32[]{:S(2)}, u32[]{:S(2)}) async-start(bf16[1,4,264,16,4]{2,3,4,0,1:T(8,128)(2,1)} %copy.71), calls=%async_computation.1 | async-start | bytes 393216 | tf_op jit(solution)/shard_map/all_to_all | solution.py:145
  244.4 30.7 %all-to-all-start.2 = ((bf16[1,4,264,4,128]{4,3,2,0,1:T(4,128)(2,1)}), bf16[1,4,264,4,128]{4,3,2,0,1:T(4,128)(2,1)S(1)}, u32[]{:S(2)}, u32[]{:S(2)}) async-start(bf16[1,4,264,4,128]{4,3,2,0,1:T(4,128)(2,1)} %bitcast.70), calls=%async_computation.2 | async-start | bytes 2162688 | tf_op jit(solution)/shard_map/all_to_all | solution.py:144
  249.6 70.6 %reduce-scatter.4.cloned.1.call-start = ((), (), s32[]{:S(2)}) async-start(), calls=%async_computation.6 | async-start | bytes 737280
  287.5 3.2 collective-permute-start.20
  288.8 6.2 %collective-permute-start.21 = (bf16[1,1,256,128]{3,2,1,0:T(8,128)(2,1)S(1)}, bf16[1,1,256,128]{3,2,1,0:T(8,128)(2,1)S(1)}, u32[]{:S(2)}, u32[]{:S(2)}) collective-permute-start(bf16[1,1,256,128]{3,2,1,0:T(8,128)(2,1)S(1)} %get-tuple-element.124), channel_id=1, source_target_pairs={{2,0},{4,2},{6,4},{3,1},{5,3},{7,5},{10,8},{12,10},{14,12},{11,9},... | collective-permute-start | bytes 196616 | tf_op jit(solution)/shard_map/ppermute | solution.py:23
  298.5 23.7 %copy-start.7 = (bf16[1152,128]{1,0:T(8,128)(2,1)S(1)}, bf16[1152,128]{1,0:T(8,128)(2,1)}, u32[]{:S(2)}) copy-start(bf16[1152,128]{1,0:T(8,128)(2,1)} %param.22) | copy-start | bytes 884740
  298.5 78.1 %all-reduce.16.cloned.1.call-start = ((), (), s32[]{:S(2)}) async-start(), calls=%async_computation.5 | async-start | bytes 1179648 | tf_op jit(solution)/shard_map/psum | solution.py:196
  (4 other events, 8.9 us)
Sparse Core Ops, SparseCore 0:
  131.3 46.6 all-reduce.13
  298.7 21.4 reduce-scatter.3
  323.3 53.2 all-reduce.15
where the time goes:
time: 387 us; the launch traced here: 385 us
  waiting for transfers between devices  190 us (49%)
  starting transfers between devices  77.4 us (20%)
  local copies, waits for them, and re-layouts  69.8 us (18%)
  matrix products  18.6 us (5%)
  between operations  14.9 us (4%)
  other arithmetic  14.7 us (4%)
    psum x1, waiting for transfers between devices, body(): conv_grad = lax.psum(grad_share, ('phase', 'dp'))  52.9 us
    psum x1, waiting for transfers between devices, from_root(): return lax.psum(block, axis)  36.8 us
    ppermute x8, waiting for transfers between devices, extended(): lax.ppermute(head, axis, [((i + 1) % count, i) for i in range(ends)])  31.1 us
    ppermute x6, starting transfers between devices, passed_along(): return lax.ppermute(block, axis, route)  27.9 us
    scatter x1, local copies, waits for them, and re-layouts, body(): send_ctx = jnp.zeros((samples_dev, tile_count * capacity, BLK, channels),...  26.6 us
    ppermute x8, starting transfers between devices, extended(): lax.ppermute(tail, axis, [(i, (i + 1) % count) for i in range(ends)])  25.9 us
    all_to_all x1, waiting for transfers between devices, body(): lax.all_to_all(send_ctx, 'tile', split_axis=1, concat_axis=1, tiled=True)  24.5 us
    unnamed x4, waiting for transfers between devices  21.7 us
  transfers between devices with their start and end apart: 28, of which 25 were waited for; matrix products, arithmetic and copies ran while one was open for 19% of the time, Pallas kernels for 0%

commit v1 on v0

--- a/solution.py
+++ b/solution.py
@@ -1,6 +1,10 @@
+import functools
+
 import jax
 import jax.numpy as jnp
 from jax import lax
+from jax.experimental import pallas as pl
+from jax.experimental.pallas import tpu as pltpu
 from jax.sharding import PartitionSpec as P
 
 NSEG = 2
@@ -197,9 +201,331 @@
     return (encoded, conv_grad)
 
 
+MESH = pl.DeviceIdType.MESH
+NT = (((1,), (1,)), ((), ()))
+TN = (((0,), (0,)), ((), ()))
+F32 = jnp.float32
+BF16 = jnp.bfloat16
+
+
+def with_side_columns(block, width):
+    rows = block.shape[0]
+    wide = block.astype(F32)
+    col = lax.broadcasted_iota(jnp.int32, block.shape, 0) % width
+    before = jnp.where(col == 0, 0.0, pltpu.roll(wide, 1, 0))
+    after = jnp.where(col == width - 1, 0.0, pltpu.roll(wide, rows - 1, 0))
+    return before.astype(BF16), block, after.astype(BF16)
+
+
+def fused_kernel(
+    dims,
+    cam_ref, w_ref, dw_ref, slots_ref, code_ref, bw_ref, cot_ref,
+    enc_ref, grad_ref,
+    x_ref, z_ref, wall_ref, codes_ref, acc_w, wt_ref, wr_ref, acc_ref, zb_ref,
+    gpart, gsend, grecv_a, gsum, gsend_b, grecv_b, grecv_c, gfin, gfin_other,
+    local_sem, row_send, row_recv, code_send, code_recv, w_send, w_recv, f_send, f_recv,
+    wt_send, wt_recv, a_send, a_recv, b_send, b_recv, c_send, c_recv, d_send, d_recv,
+):
+    phases, tiles, width, slots, bins, seg, grid_rows, grid_cols, scale = dims
+    ph, ti, dp = lax.axis_index("phase"), lax.axis_index("tile"), lax.axis_index("dp")
+    other = 1 - dp
+    pos = cam_ref.shape[1]
+    channels = cam_ref.shape[2]
+    lanes = code_ref.shape[1]
+    half = w_ref.shape[0] // 2
+    cols3 = 3 * channels
+
+    def tile_peer(k):
+        return (ph, lax.rem(ti + k, tiles), dp)
+
+    def phase_peer(k):
+        return (lax.rem(ph + k, phases), ti, dp)
+
+    partner = (ph, ti, other)
+
+    barrier = pltpu.get_barrier_semaphore()
+    for k in range(1, tiles):
+        pl.semaphore_signal(barrier, inc=1, device_id=tile_peer(k), device_id_type=MESH)
+    for k in range(1, phases):
+        pl.semaphore_signal(barrier, inc=1, device_id=phase_peer(k), device_id_type=MESH)
+    pl.semaphore_signal(barrier, inc=1, device_id=partner, device_id_type=MESH)
+    pl.semaphore_wait(barrier, tiles - 1 + phases - 1 + 1)
+
+    def remote(src, dst, send, recv, device):
+        copy = pltpu.make_async_remote_copy(
+            src_ref=src, dst_ref=dst, send_sem=send, recv_sem=recv,
+            device_id=device, device_id_type=MESH,
+        )
+        copy.start()
+        return copy
+
+    own_rows = pl.ds(pl.multiple_of(ti * pos, 16), pos)
+    own_lanes = pl.ds(pl.multiple_of(ti * lanes, 128), lanes)
+    own_half = pl.ds(pl.multiple_of(dp * half, 16), half)
+    w_copies = [
+        remote(w_ref.at[own_half], wall_ref.at[ph, own_half], w_send.at[k], w_recv.at[k], phase_peer(k))
+        for k in range(1, phases)
+    ]
+    row_copies = [
+        remote(cam_ref.at[ph], x_ref.at[own_rows], row_send.at[k], row_recv.at[k], tile_peer(k))
+        for k in range(1, tiles)
+    ]
+    code_copies = [
+        remote(code_ref, codes_ref.at[:, own_lanes], code_send.at[k], code_recv.at[k], tile_peer(k))
+        for k in range(1, tiles)
+    ]
+    own = [
+        pltpu.make_async_copy(cam_ref.at[ph], x_ref.at[own_rows], local_sem.at[0]),
+        pltpu.make_async_copy(code_ref, codes_ref.at[:, own_lanes], local_sem.at[1]),
+        pltpu.make_async_copy(w_ref, wall_ref.at[ph], local_sem.at[2]),
+    ]
+    for copy in own:
+        copy.start()
+
+    edge = jnp.zeros((pos, cols3), BF16)
+    z_ref[pl.ds(0, pos), :] = edge
+    z_ref[pl.ds((tiles + 1) * pos, pos), :] = edge
+    acc_ref[...] = jnp.zeros_like(acc_ref)
+    acc_w[...] = jnp.zeros_like(acc_w)
+
+    forwards = []
+    for k in range(1, phases):
+        w_copies[k - 1].wait_recv()
+        source = lax.rem(ph - k + phases, phases)
+        forwards.append(
+            remote(wall_ref.at[source, own_half], wall_ref.at[source, own_half],
+                   f_send.at[k], f_recv.at[k], partner)
+        )
+    for copy in own + row_copies + code_copies + forwards:
+        copy.wait()
+    for copy in w_copies:
+        copy.wait_send()
+
+    @pl.loop(0, phases)
+    def _(s):
+        @pl.loop(0, tiles)
+        def _(u):
+            rows = x_ref[pl.ds(pl.multiple_of(u * pos, 16), pos), :]
+            at = pl.ds(pl.multiple_of((u + 1) * pos, 16), pos)
+            for e, part in enumerate(with_side_columns(rows, width)):
+                z_ref[at, e * channels : (e + 1) * channels] = part
+
+        @pl.loop(0, tiles)
+        def _(u):
+            at = pl.ds(pl.multiple_of(u * pos, 16), pos)
+            hidden = jnp.zeros((pos, channels), F32)
+            for a in range(3):
+                hidden += jnp.dot(
+                    z_ref[pl.ds(pl.multiple_of((u + a) * pos, 16), pos), :],
+                    wall_ref[s, a * cols3 : (a + 1) * cols3, :],
+                    preferred_element_type=F32,
+                )
+            x_ref[at, :] = (x_ref[at, :].astype(F32) + hidden * jax.nn.sigmoid(hidden)).astype(BF16)
+
+    logits = jnp.dot(x_ref[own_rows, :], dw_ref[...], preferred_element_type=F32)
+    lane = lax.broadcasted_iota(jnp.int32, logits.shape, 1)
+    inside = (lane % 128) < seg
+    raised = jnp.where(inside, jnp.exp(BOUND * jnp.tanh(logits / BOUND)), 0.0)
+    prob = raised / jnp.sum(raised, axis=1, keepdims=True)
+    half_of = lax.broadcasted_iota(jnp.int32, (bins, 128), 0) // 128
+    target_col = lax.broadcasted_iota(jnp.int32, (bins, 128), 1)
+    summed = jnp.zeros((pos, 128), F32)
+    for t in range(slots):
+        chosen = jnp.where(slots_ref[...] == t, prob, 0.0).astype(BF16)
+        into = jnp.where(target_col == half_of * slots + t, 1.0, 0.0).astype(BF16)
+        summed += jnp.dot(chosen, into, preferred_element_type=F32)
+    acc_w[pl.ds(0, pos), :] = summed.astype(BF16)
+    names = NSEG * slots
+    pick = jnp.where(
+        lax.broadcasted_iota(jnp.int32, (names, 128), 0) == lax.broadcasted_iota(jnp.int32, (names, 128), 1),
+        1.0, 0.0,
+    ).astype(BF16)
+    wt_ref[ti] = lax.dot_general(pick, acc_w[...], NT, preferred_element_type=F32).astype(BF16)
+    wt_copies = [
+        remote(wt_ref.at[ti], wt_ref.at[ti], wt_send.at[k], wt_recv.at[k], tile_peer(k))
+        for k in range(1, tiles)
+    ]
+    for copy in wt_copies:
+        copy.wait()
+
+    chunk = 16
+    chunk_rows = chunk * names
+    chunk_pos = chunk * BLK
+    spread = jnp.where(
+        lax.broadcasted_iota(jnp.int32, (names, chunk_rows), 1) % names
+        == lax.broadcasted_iota(jnp.int32, (names, chunk_rows), 0),
+        1.0, 0.0,
+    ).astype(BF16)
+
+    @pl.loop(0, tiles)
+    def _(u):
+        back = wt_ref[u].astype(F32).T.astype(BF16)
+        tiled = jnp.dot(back[:pos], spread, preferred_element_type=F32)
+        wr_ref[pl.ds(pl.multiple_of(u * pos, 16), pos), :] = tiled.astype(BF16)
+
+    shape = (chunk_pos, chunk_rows)
+    same = jnp.where(
+        lax.broadcasted_iota(jnp.int32, shape, 0) // BLK == lax.broadcasted_iota(jnp.int32, shape, 1) // names,
+        1.0, 0.0,
+    ).astype(BF16)
+    window = grid_rows + 2
+
+    @pl.loop(0, tiles * pos // chunk_pos)
+    def _(c):
+        at = pl.ds(pl.multiple_of(c * chunk_pos, 16), chunk_pos)
+        weights = wr_ref[at, :] * same
+        pooled = lax.dot_general(x_ref[at, :], weights, TN, preferred_element_type=F32).astype(BF16)
+        cell = codes_ref[:, pl.ds(pl.multiple_of(c * chunk_rows, 128), chunk_rows)]
+        cell = cell - (ti * grid_rows - 1) * grid_cols
+        row = cell >> 8
+        column = cell & (grid_cols - 1)
+        marks = jnp.where(
+            lax.broadcasted_iota(jnp.int32, (grid_cols, chunk_rows), 0) == column, 1.0, 0.0
+        ).astype(BF16)
+        parts = [pooled * jnp.where(row == y, 1.0, 0.0).astype(BF16) for y in range(window)]
+        acc_ref[...] += lax.dot_general(
+            jnp.concatenate(parts, axis=0), marks, NT, preferred_element_type=F32
+        )
+
+    for y in range(window):
+        line = acc_ref[y * channels : (y + 1) * channels, :].T.astype(BF16)
+        for e, part in enumerate(with_side_columns(line, grid_cols)):
+            zb_ref[y * grid_cols : (y + 1) * grid_cols, e * channels : (e + 1) * channels] = part
+
+    cells = grid_rows * grid_cols
+    upstream = cot_ref[...].astype(F32).T.astype(BF16)
+    for a in range(3):
+        term = scale * jnp.dot(
+            upstream, zb_ref[a * grid_cols : a * grid_cols + cells, :], preferred_element_type=F32
+        )
+        for t in range(tiles):
+            for d in range(2):
+                piece = term[(2 * t + d) * 16 : (2 * t + d + 1) * 16]
+                gpart[d, t, :, a * cols3 : (a + 1) * cols3] = piece
+                gsend[d, t, :, a * cols3 : (a + 1) * cols3] = piece.astype(BF16)
+    to_partner = remote(gsend.at[other], grecv_a, a_send, a_recv, partner)
+
+    for y in range(grid_rows):
+        mixed = zb_ref[(y + 1) * grid_cols : (y + 2) * grid_cols, channels : 2 * channels].astype(F32)
+        for a in range(3):
+            mixed += jnp.dot(
+                zb_ref[(y + a) * grid_cols : (y + a + 1) * grid_cols, :],
+                bw_ref[a * cols3 : (a + 1) * cols3, :],
+                preferred_element_type=F32,
+            )
+        enc_ref[y * grid_cols : (y + 1) * grid_cols, :] = mixed.astype(BF16)
+
+    to_partner.wait()
+    for t in range(tiles):
+        total = gpart[dp, t] + grecv_a[t].astype(F32)
+        gsum[t] = total
+        gsend_b[t] = total.astype(BF16)
+    b_copies = [
+        remote(gsend_b.at[lax.rem(ti + k, tiles)], grecv_b.at[ti], b_send.at[k], b_recv.at[k], tile_peer(k))
+        for k in range(1, tiles)
+    ]
+    for copy in b_copies:
+        copy.wait()
+    total = gsum[ti]
+    for k in range(1, tiles):
+        total += grecv_b[lax.rem(ti + k, tiles)].astype(F32)
+    grecv_c[ph] = total.astype(BF16)
+    c_copies = [
+        remote(grecv_c.at[ph], grecv_c.at[ph], c_send.at[k], c_recv.at[k], phase_peer(k))
+        for k in range(1, phases)
+    ]
+    for copy in c_copies:
+        copy.wait()
+    total = grecv_c[0].astype(F32)
+    for p in range(1, phases):
+        total += grecv_c[p].astype(F32)
+    gfin[...] = total
+    last = remote(gfin, gfin_other, d_send, d_recv, partner)
+    grad_ref[dp] = total
+    last.wait()
+    grad_ref[other] = gfin_other[...]
+
+
+def fused_body(camera_feats, backbone_w, depth_w, block_tile, point_slot, block_cells, bev_w, cotangent):
+    phases, tiles = lax.axis_size("phase"), lax.axis_size("tile")
+    micro, _, cams, _, width, channels = camera_feats.shape
+    pos = cams * width
+    groups = pos // BLK
+    seg = depth_w.shape[1] // NSEG
+    slots = block_cells.shape[-1]
+    grid_rows, grid_cols = cotangent.shape[2:4]
+    cells = grid_rows * grid_cols
+    side = [(0, 0), (0, 0), (0, 128 - seg)]
+    bins = NSEG * 128
+    heads = jnp.pad(depth_w.reshape(channels, NSEG, seg), side).reshape(channels, bins)
+    point = point_slot.reshape(groups, NSEG, BLK, seg).transpose(0, 2, 1, 3).reshape(pos, NSEG, seg)
+    point = jnp.pad(point, side).reshape(pos, bins)
+    local = block_cells.reshape(groups * NSEG, slots)
+    code = block_tile.reshape(groups * NSEG, 1) * cells + local
+    code = jnp.where(local < cells, code, 1 << 24).reshape(1, groups * NSEG * slots)
+    total = micro * cotangent.shape[1] * lax.axis_size("dp") * cells * tiles
+    dims = (phases, tiles, width, slots, bins, seg, grid_rows, grid_cols, float(total) ** (-0.5))
+    rows = code.shape[1]
+    cols = 9 * channels
+    pad_pos = -(-pos // 128) * 128
+    dma = pltpu.SemaphoreType.DMA
+    vmem = pl.BlockSpec(memory_space=pltpu.VMEM)
+    scratch = [
+        pltpu.VMEM((tiles * pos, channels), BF16),
+        pltpu.VMEM(((tiles + 2) * pos, 3 * channels), BF16),
+        pltpu.VMEM((phases, cols, channels), BF16),
+        pltpu.VMEM((1, tiles * rows), jnp.int32),
+        pltpu.VMEM((pad_pos, 128), BF16),
+        pltpu.VMEM((tiles, NSEG * slots, pad_pos), BF16),
+        pltpu.VMEM((tiles * pos, 16 * NSEG * slots), BF16),
+        pltpu.VMEM(((grid_rows + 2) * channels, grid_cols), F32),
+        pltpu.VMEM(((grid_rows + 2) * grid_cols, 3 * channels), BF16),
+        pltpu.VMEM((2, tiles, 16, cols), F32),
+        pltpu.VMEM((2, tiles, 16, cols), BF16),
+        pltpu.VMEM((tiles, 16, cols), BF16),
+        pltpu.VMEM((tiles, 16, cols), F32),
+        pltpu.VMEM((tiles, 16, cols), BF16),
+        pltpu.VMEM((tiles, 16, cols), BF16),
+        pltpu.VMEM((phases, 16, cols), BF16),
+        pltpu.VMEM((16, cols), F32),
+        pltpu.VMEM((16, cols), F32),
+        dma((3,)),
+        dma((tiles,)), dma((tiles,)), dma((tiles,)), dma((tiles,)),
+        dma((phases,)), dma((phases,)), dma((phases,)), dma((phases,)),
+        dma((tiles,)), dma((tiles,)),
+        dma(()), dma(()),
+        dma((tiles,)), dma((tiles,)),
+        dma((phases,)), dma((phases,)),
+        dma(()), dma(()),
+    ]
+    encoded, grad = pl.pallas_call(
+        functools.partial(fused_kernel, dims),
+        out_shape=(
+            jax.ShapeDtypeStruct((cells, channels), BF16),
+            jax.ShapeDtypeStruct((2, 16, cols), F32),
+        ),
+        in_specs=[vmem] * 7,
+        out_specs=(vmem, vmem),
+        scratch_shapes=scratch,
+        compiler_params=pltpu.CompilerParams(
+            collective_id=0, has_side_effects=True, vmem_limit_bytes=48 * 1024 * 1024
+        ),
+        name="lift_splat",
+    )(
+        camera_feats.reshape(micro, pos, channels),
+        backbone_w[0],
+        heads,
+        point,
+        code,
+        bev_w,
+        cotangent.reshape(cells, channels),
+    )
+    return encoded.reshape(cotangent.shape), grad.reshape(32, cols)
+
+
 def solution(mesh):
     return jax.shard_map(
-        body,
+        fused_body if mesh.shape["tile"] == 4 else body,
         mesh=mesh,
         in_specs=(
             P(None, "dp", None, "tile", None, None),

time: 387 us -> 75.4 us (0.19)
  waiting for transfers between devices: 190 us -> 0 us
  starting transfers between devices: 77.4 us -> 0 us
  Pallas kernels: 0 us -> 69.3 us
  local copies, waits for them, and re-layouts: 69.8 us -> 4.96 us
  matrix products: 18.6 us -> 0 us
  other arithmetic: 14.7 us -> 0.05 us
  between operations: 14.9 us -> 0.82 us
    psum x2 -> x0, waiting for transfers between devices: 89.8 us -> none  [the longest x1 52.9 us: body(): conv_grad = lax.psum(grad_share, ('phase', 'dp'))]
    pallas_call x0 -> x1, Pallas kernels: none -> 69.3 us  [fused_body(): pl.pallas_call(functools.partial(fused_kernel, dims), out_shape=(jax.Shap...]
    ppermute x22 -> x0, starting transfers between devices: 64.1 us -> none  [the longest x6 27.9 us: passed_along(): return lax.ppermute(block, axis, route)]
    ppermute x22 -> x0, waiting for transfers between devices: 53.6 us -> none  [the longest x8 31.1 us: extended(): lax.ppermute(head, axis, [((i + 1) % count, i) for i in range(ends)])]
    scatter x4 -> x0, local copies, waits for them, and re-layouts: 36.6 us -> none  [the longest x1 26.6 us: body(): send_ctx = jnp.zeros((samples_dev, tile_count * capacity, BLK, channels),...]
    all_to_all x3 -> x0, waiting for transfers between devices: 24.5 us -> none  [the longest x1 24.5 us: body(): lax.all_to_all(send_ctx, 'tile', split_axis=1, concat_axis=1, tiled=True)]
    unnamed x4 -> x0, waiting for transfers between devices: 21.7 us -> none
    dot_general x12 -> x0, matrix products: 18.6 us -> none  [the longest x1 10.5 us: splat_group(): jnp.einsum('sxr,src->sxc', one_hot, part_pooled, preferred_element_type=j...]
  transfers between devices with their start and end apart: 28 -> 0, of which waited for: 25 -> 0; matrix products, arithmetic and copies ran while one was open for 19% -> 0% of each run, Pallas kernels for 0% -> 0%
where the time goes in v1:
time: 75.4 us; the launch traced here: 75.2 us
  Pallas kernels  69.3 us (92%)
  local copies, waits for them, and re-layouts  4.96 us (7%)
  between operations  0.82 us (1%)
    pallas_call x1, Pallas kernels, fused_body(): pl.pallas_call(functools.partial(fused_kernel, dims), out_shape=(jax.Shap...  69.3 us
    unnamed x19, local copies, waits for them, and re-layouts  2.97 us

profile of v1, /device:TPU:0, one launch (start us, length us, event | category | flops | bytes accessed | tf_op | source)
XLA Modules:
  0.0 75.2 jit_solution(12236364460339128160)
XLA Ops:
  0.6 1.2 %reshape.79 = s32[132,2,4,59]{3,2,1,0:T(4,128)S(1)} reshape(s32[1,1,264,236]{3,2,1,0:T(8,128)} %param.12) | data formatting | bytes 498432 | tf_op jit(solution)/shard_map/reshape | solution.py:461
  1.9 0.1 copy.16
  2.0 0.3 copy.20
  2.3 0.2 pad.9.clone
  2.5 0.0 copy-start.6
  2.5 0.0 copy-start.5
  2.5 0.0 copy-start.2
  2.5 0.0 copy-start.3
  2.6 0.0 copy-start
  2.6 0.6 copy-done.6
  3.2 0.1 add.21
  3.3 0.0 copy-start.4
  3.3 0.1 add.22
  3.4 0.0 copy-done.5
  3.4 0.0 copy-start.1
  3.4 0.1 copy.18
  3.5 0.1 reshape.82
  3.7 0.3 copy-done.4
  4.1 0.1 copy.19.dw_ref
  4.2 0.0 copy-done.2
  4.2 0.0 copy-done.3
  4.2 0.0 copy-done
  4.2 0.2 copy-done.1
  4.5 69.3 %lift_splat.1 = (bf16[1024,128]{1,0:T(8,128)(2,1)S(1)}, f32[2,16,1152]{2,1,0:T(8,128)S(1)}) custom-call(bf16[4,528,128]{2,1,0:T(8,128)(2,1)S(1)} %bitcast.19, bf16[1152,128]{1,0:T(8,128)(2,1)S(1)} %bitcast.20, bf16[128,256]{1,0:T(8,128)(2,1)S(1)} %copy.19.dw_ref, s32[528,256]{1,0:T(8,128)S(1)} %bitcast.18, s32[1,4224]{1,0:T(1,128)S(1)} %compare_select_fusion.code_ref, ...), custom_call_target="tpu_custom_call" | custom-call | tf_op jit(solution)/shard_map/lift_splat/pallas_call | solution.py:501
  73.8 0.7 copy.26
  74.5 0.7 copy.27
  (5 shorter events, 0.1 us)
Async XLA Ops:
  2.5 0.7 copy-start.6
  2.5 0.9 %copy-start.5 = (s32[1,1,264,16]{2,3,1,0:T(8,128)S(1)}, s32[1,1,264,16]{2,3,1,0:T(8,128)}, u32[]{:S(2)}) copy-start(s32[1,1,264,16]{2,3,1,0:T(8,128)} %param.13) | copy-start | bytes 50692
  2.5 1.7 %copy-start.2 = (bf16[1152,128]{1,0:T(8,128)(2,1)S(1)}, bf16[1152,128]{1,0:T(8,128)(2,1)}, u32[]{:S(2)}) copy-start(bf16[1152,128]{1,0:T(8,128)(2,1)} %bw_ref.1) | copy-start | bytes 884740
  2.5 1.7 %copy-start.3 = (bf16[1,1,4,256,128]{4,3,2,1,0:T(8,128)(2,1)S(1)}, bf16[1,1,4,256,128]{4,3,2,1,0:T(8,128)(2,1)}, u32[]{:S(2)}) copy-start(bf16[1,1,4,256,128]{4,3,2,1,0:T(8,128)(2,1)} %param.15) | copy-start | bytes 786436
  2.6 1.6 %copy-start = (bf16[4,1,3,1,176,128]{5,4,3,2,1,0:T(8,128)(2,1)S(1)}, bf16[4,1,3,1,176,128]{5,4,3,2,1,0:T(8,128)(2,1)}, u32[]{:S(2)}) copy-start(bf16[4,1,3,1,176,128]{5,4,3,2,1,0:T(8,128)(2,1)} %param.8) | copy-start | bytes 1622020
  3.3 0.8 %copy-start.4 = (bf16[128,118]{0,1:T(8,128)(2,1)S(1)}, bf16[128,118]{0,1:T(8,128)(2,1)}, u32[]{:S(2)}) copy-start(bf16[128,118]{0,1:T(8,128)(2,1)} %param.10) | copy-start | bytes 90628
  3.4 1.0 %copy-start.1 = (bf16[1,1152,128]{2,1,0:T(8,128)(2,1)S(1)}, bf16[1,1152,128]{2,1,0:T(8,128)(2,1)}, u32[]{:S(2)}) copy-start(bf16[1,1152,128]{2,1,0:T(8,128)(2,1)} %param.9) | copy-start | bytes 884740

commit v2 on v1

--- a/solution.py
+++ b/solution.py
@@ -221,7 +221,7 @@
     dims,
     cam_ref, w_ref, dw_ref, slots_ref, code_ref, bw_ref, cot_ref,
     enc_ref, grad_ref,
-    x_ref, z_ref, wall_ref, codes_ref, acc_w, wt_ref, wr_ref, acc_ref, zb_ref,
+    x_ref, z_ref, wall_ref, codes_ref, acc_w, wt_ref, back_ref, same_ref, up_ref, acc_ref, zb_ref,
     gpart, gsend, grecv_a, gsum, gsend_b, grecv_b, grecv_c, gfin, gfin_other,
     local_sem, row_send, row_recv, code_send, code_recv, w_send, w_recv, f_send, f_recv,
     wt_send, wt_recv, a_send, a_recv, b_send, b_recv, c_send, c_recv, d_send, d_recv,
@@ -288,6 +288,7 @@
     acc_ref[...] = jnp.zeros_like(acc_ref)
     acc_w[...] = jnp.zeros_like(acc_w)
 
+    up_ref[...] = cot_ref[...].astype(F32).T.astype(BF16)
     forwards = []
     for k in range(1, phases):
         w_copies[k - 1].wait_recv()
@@ -303,23 +304,20 @@
 
     @pl.loop(0, phases)
     def _(s):
-        @pl.loop(0, tiles)
+        @pl.loop(0, tiles, unroll=2)
         def _(u):
             rows = x_ref[pl.ds(pl.multiple_of(u * pos, 16), pos), :]
             at = pl.ds(pl.multiple_of((u + 1) * pos, 16), pos)
             for e, part in enumerate(with_side_columns(rows, width)):
                 z_ref[at, e * channels : (e + 1) * channels] = part
 
-        @pl.loop(0, tiles)
+        @pl.loop(0, tiles, unroll=2)
         def _(u):
             at = pl.ds(pl.multiple_of(u * pos, 16), pos)
-            hidden = jnp.zeros((pos, channels), F32)
-            for a in range(3):
-                hidden += jnp.dot(
-                    z_ref[pl.ds(pl.multiple_of((u + a) * pos, 16), pos), :],
-                    wall_ref[s, a * cols3 : (a + 1) * cols3, :],
-                    preferred_element_type=F32,
-                )
+            patches = jnp.concatenate(
+                [z_ref[pl.ds(pl.multiple_of((u + a) * pos, 16), pos), :] for a in range(3)], axis=1
+            )
+            hidden = jnp.dot(patches, wall_ref[s], preferred_element_type=F32)
             x_ref[at, :] = (x_ref[at, :].astype(F32) + hidden * jax.nn.sigmoid(hidden)).astype(BF16)
 
     logits = jnp.dot(x_ref[own_rows, :], dw_ref[...], preferred_element_type=F32)
@@ -341,51 +339,56 @@
         1.0, 0.0,
     ).astype(BF16)
     wt_ref[ti] = lax.dot_general(pick, acc_w[...], NT, preferred_element_type=F32).astype(BF16)
-    wt_copies = [
+    for k in range(1, tiles):
         remote(wt_ref.at[ti], wt_ref.at[ti], wt_send.at[k], wt_recv.at[k], tile_peer(k))
-        for k in range(1, tiles)
-    ]
-    for copy in wt_copies:
-        copy.wait()
-
-    chunk = 16
-    chunk_rows = chunk * names
-    chunk_pos = chunk * BLK
+
+    chunk_pos = width
+    chunk_rows = chunk_pos // BLK * names
     spread = jnp.where(
         lax.broadcasted_iota(jnp.int32, (names, chunk_rows), 1) % names
         == lax.broadcasted_iota(jnp.int32, (names, chunk_rows), 0),
         1.0, 0.0,
     ).astype(BF16)
-
-    @pl.loop(0, tiles)
-    def _(u):
-        back = wt_ref[u].astype(F32).T.astype(BF16)
-        tiled = jnp.dot(back[:pos], spread, preferred_element_type=F32)
-        wr_ref[pl.ds(pl.multiple_of(u * pos, 16), pos), :] = tiled.astype(BF16)
-
     shape = (chunk_pos, chunk_rows)
-    same = jnp.where(
+    same_ref[...] = jnp.where(
         lax.broadcasted_iota(jnp.int32, shape, 0) // BLK == lax.broadcasted_iota(jnp.int32, shape, 1) // names,
         1.0, 0.0,
     ).astype(BF16)
     window = grid_rows + 2
 
-    @pl.loop(0, tiles * pos // chunk_pos)
-    def _(c):
-        at = pl.ds(pl.multiple_of(c * chunk_pos, 16), chunk_pos)
-        weights = wr_ref[at, :] * same
-        pooled = lax.dot_general(x_ref[at, :], weights, TN, preferred_element_type=F32).astype(BF16)
-        cell = codes_ref[:, pl.ds(pl.multiple_of(c * chunk_rows, 128), chunk_rows)]
-        cell = cell - (ti * grid_rows - 1) * grid_cols
-        row = cell >> 8
-        column = cell & (grid_cols - 1)
-        marks = jnp.where(
-            lax.broadcasted_iota(jnp.int32, (grid_cols, chunk_rows), 0) == column, 1.0, 0.0
-        ).astype(BF16)
-        parts = [pooled * jnp.where(row == y, 1.0, 0.0).astype(BF16) for y in range(window)]
-        acc_ref[...] += lax.dot_general(
-            jnp.concatenate(parts, axis=0), marks, NT, preferred_element_type=F32
-        )
+    def add_blocks(u):
+        back_ref[...] = wt_ref[u].astype(F32).T.astype(BF16)
+
+        @pl.loop(0, pos // chunk_pos)
+        def _(c):
+            here = pl.ds(pl.multiple_of(c * chunk_pos, 16), chunk_pos)
+            at = pl.ds(pl.multiple_of(u * pos + c * chunk_pos, 16), chunk_pos)
+            tiled = jnp.dot(back_ref[here, :], spread, preferred_element_type=F32)
+            weights = tiled.astype(BF16) * same_ref[...]
+            pooled = lax.dot_general(x_ref[at, :], weights, TN, preferred_element_type=F32).astype(BF16)
+            cell = codes_ref[:, pl.ds(pl.multiple_of(u * lanes + c * chunk_rows, 128), chunk_rows)]
+            cell = cell - (ti * grid_rows - 1) * grid_cols
+            row = cell >> 8
+            column = cell & (grid_cols - 1)
+            marks = jnp.where(
+                lax.broadcasted_iota(jnp.int32, (grid_cols, chunk_rows), 0) == column, 1.0, 0.0
+            ).astype(BF16)
+            parts = [pooled * jnp.where(row == y, 1.0, 0.0).astype(BF16) for y in range(window)]
+            acc_ref[...] += lax.dot_general(
+                jnp.concatenate(parts, axis=0), marks, NT, preferred_element_type=F32
+            )
+
+    @pl.loop(0, tiles)
+    def _(d):
+        @pl.when(d > 0)
+        def _():
+            pltpu.make_async_remote_copy(
+                src_ref=wt_ref.at[ti], dst_ref=wt_ref.at[ti],
+                send_sem=wt_send.at[d], recv_sem=wt_recv.at[d],
+                device_id=tile_peer(d), device_id_type=MESH,
+            ).wait()
+
+        add_blocks(lax.rem(ti + tiles - d, tiles))
 
     for y in range(window):
         line = acc_ref[y * channels : (y + 1) * channels, :].T.astype(BF16)
@@ -393,10 +396,9 @@
             zb_ref[y * grid_cols : (y + 1) * grid_cols, e * channels : (e + 1) * channels] = part
 
     cells = grid_rows * grid_cols
-    upstream = cot_ref[...].astype(F32).T.astype(BF16)
     for a in range(3):
         term = scale * jnp.dot(
-            upstream, zb_ref[a * grid_cols : a * grid_cols + cells, :], preferred_element_type=F32
+            up_ref[...], zb_ref[a * grid_cols : a * grid_cols + cells, :], preferred_element_type=F32
         )
         for t in range(tiles):
             for d in range(2):
@@ -405,16 +407,17 @@
                 gsend[d, t, :, a * cols3 : (a + 1) * cols3] = piece.astype(BF16)
     to_partner = remote(gsend.at[other], grecv_a, a_send, a_recv, partner)
 
-    for y in range(grid_rows):
-        mixed = zb_ref[(y + 1) * grid_cols : (y + 2) * grid_cols, channels : 2 * channels].astype(F32)
-        for a in range(3):
-            mixed += jnp.dot(
-                zb_ref[(y + a) * grid_cols : (y + a + 1) * grid_cols, :],
-                bw_ref[a * cols3 : (a + 1) * cols3, :],
-                preferred_element_type=F32,
-            )
+    def encode(y):
+        patches = jnp.concatenate(
+            [zb_ref[(y + a) * grid_cols : (y + a + 1) * grid_cols, :] for a in range(3)], axis=1
+        )
+        own_row = zb_ref[(y + 1) * grid_cols : (y + 2) * grid_cols, channels : 2 * channels]
+        mixed = own_row.astype(F32) + jnp.dot(patches, bw_ref[...], preferred_element_type=F32)
         enc_ref[y * grid_cols : (y + 1) * grid_cols, :] = mixed.astype(BF16)
 
+    quarter = grid_rows // 4
+    for y in range(quarter):
+        encode(y)
     to_partner.wait()
     for t in range(tiles):
         total = gpart[dp, t] + grecv_a[t].astype(F32)
@@ -424,6 +427,8 @@
         remote(gsend_b.at[lax.rem(ti + k, tiles)], grecv_b.at[ti], b_send.at[k], b_recv.at[k], tile_peer(k))
         for k in range(1, tiles)
     ]
+    for y in range(quarter, 3 * quarter):
+        encode(y)
     for copy in b_copies:
         copy.wait()
     total = gsum[ti]
@@ -434,6 +439,8 @@
         remote(grecv_c.at[ph], grecv_c.at[ph], c_send.at[k], c_recv.at[k], phase_peer(k))
         for k in range(1, phases)
     ]
+    for y in range(3 * quarter, grid_rows):
+        encode(y)
     for copy in c_copies:
         copy.wait()
     total = grecv_c[0].astype(F32)
@@ -477,7 +484,9 @@
         pltpu.VMEM((1, tiles * rows), jnp.int32),
         pltpu.VMEM((pad_pos, 128), BF16),
         pltpu.VMEM((tiles, NSEG * slots, pad_pos), BF16),
-        pltpu.VMEM((tiles * pos, 16 * NSEG * slots), BF16),
+        pltpu.VMEM((pad_pos, NSEG * slots), BF16),
+        pltpu.VMEM((width, width // BLK * NSEG * slots), BF16),
+        pltpu.VMEM((channels, cells), BF16),
         pltpu.VMEM(((grid_rows + 2) * channels, grid_cols), F32),
         pltpu.VMEM(((grid_rows + 2) * grid_cols, 3 * channels), BF16),
         pltpu.VMEM((2, tiles, 16, cols), F32),

time: 75.4 us -> 63.9 us (0.85)
  Pallas kernels: 69.3 us -> 57.9 us
    pallas_call x1, Pallas kernels: 69.3 us -> 57.9 us  [fused_body(): pl.pallas_call(functools.partial(fused_kernel, dims), out_shape=(jax.Shap...]
where the time goes in v2:
time: 63.9 us; the launch traced here: 63.7 us
  Pallas kernels  57.9 us (91%)
  local copies, waits for them, and re-layouts  4.96 us (8%)
  between operations  0.82 us (1%)
    pallas_call x1, Pallas kernels, fused_body(): pl.pallas_call(functools.partial(fused_kernel, dims), out_shape=(jax.Shap...  57.9 us
    unnamed x19, local copies, waits for them, and re-layouts  2.97 us

profile of v2, /device:TPU:0, one launch (start us, length us, event | category | flops | bytes accessed | tf_op | source)
XLA Modules:
  0.0 63.7 jit_solution(16364676317954432627)
XLA Ops:
  0.6 1.2 %reshape.79 = s32[132,2,4,59]{3,2,1,0:T(4,128)S(1)} reshape(s32[1,1,264,236]{3,2,1,0:T(8,128)} %param.12) | data formatting | bytes 498432 | tf_op jit(solution)/shard_map/reshape | solution.py:468
  1.9 0.1 copy.16
  2.0 0.3 copy.20
  2.3 0.2 pad.9.clone
  2.5 0.0 copy-start.6
  2.5 0.0 copy-start.5
  2.5 0.0 copy-start.2
  2.5 0.0 copy-start.3
  2.6 0.0 copy-start
  2.6 0.6 copy-done.6
  3.2 0.1 add.21
  3.3 0.0 copy-start.4
  3.3 0.1 add.22
  3.4 0.0 copy-done.5
  3.4 0.0 copy-start.1
  3.4 0.1 copy.18
  3.5 0.1 reshape.82
  3.7 0.3 copy-done.4
  4.1 0.1 copy.19.dw_ref
  4.2 0.0 copy-done.2
  4.2 0.0 copy-done.3
  4.2 0.0 copy-done
  4.2 0.2 copy-done.1
  4.5 57.9 %lift_splat.1 = (bf16[1024,128]{1,0:T(8,128)(2,1)S(1)}, f32[2,16,1152]{2,1,0:T(8,128)S(1)}) custom-call(bf16[4,528,128]{2,1,0:T(8,128)(2,1)S(1)} %bitcast.19, bf16[1152,128]{1,0:T(8,128)(2,1)S(1)} %bitcast.20, bf16[128,256]{1,0:T(8,128)(2,1)S(1)} %copy.19.dw_ref, s32[528,256]{1,0:T(8,128)S(1)} %bitcast.18, s32[1,4224]{1,0:T(1,128)S(1)} %compare_select_fusion.code_ref, ...), custom_call_target="tpu_custom_call" | custom-call | tf_op jit(solution)/shard_map/lift_splat/pallas_call | solution.py:510
  62.3 0.7 %copy.26 = bf16[1,1,4,256,128]{4,3,2,1,0:T(8,128)(2,1)} copy(bf16[1,1,4,256,128]{4,3,2,1,0:T(8,128)(2,1)S(1)} %bitcast.22) | data formatting | bytes 524288
  63.0 0.7 %copy.27 = f32[32,1152]{1,0:T(8,128)} copy(f32[32,1152]{1,0:T(8,128)S(1)} %bitcast.23) | data formatting | bytes 294912
  (5 shorter events, 0.1 us)
Async XLA Ops:
  2.5 0.7 %copy-start.6 = (s32[1,1,264,1]{2,3,1,0:T(1,128)S(1)}, s32[1,1,264,1]{2,3,1,0:T(1,128)}, u32[]{:S(2)}) copy-start(s32[1,1,264,1]{2,3,1,0:T(1,128)} %param.11) | copy-start | bytes 3172
  2.5 0.9 %copy-start.5 = (s32[1,1,264,16]{2,3,1,0:T(8,128)S(1)}, s32[1,1,264,16]{2,3,1,0:T(8,128)}, u32[]{:S(2)}) copy-start(s32[1,1,264,16]{2,3,1,0:T(8,128)} %param.13) | copy-start | bytes 50692
  2.5 1.7 %copy-start.2 = (bf16[1152,128]{1,0:T(8,128)(2,1)S(1)}, bf16[1152,128]{1,0:T(8,128)(2,1)}, u32[]{:S(2)}) copy-start(bf16[1152,128]{1,0:T(8,128)(2,1)} %bw_ref.1) | copy-start | bytes 884740
  2.5 1.7 %copy-start.3 = (bf16[1,1,4,256,128]{4,3,2,1,0:T(8,128)(2,1)S(1)}, bf16[1,1,4,256,128]{4,3,2,1,0:T(8,128)(2,1)}, u32[]{:S(2)}) copy-start(bf16[1,1,4,256,128]{4,3,2,1,0:T(8,128)(2,1)} %param.15) | copy-start | bytes 786436
  2.6 1.6 %copy-start = (bf16[4,1,3,1,176,128]{5,4,3,2,1,0:T(8,128)(2,1)S(1)}, bf16[4,1,3,1,176,128]{5,4,3,2,1,0:T(8,128)(2,1)}, u32[]{:S(2)}) copy-start(bf16[4,1,3,1,176,128]{5,4,3,2,1,0:T(8,128)(2,1)} %param.8) | copy-start | bytes 1622020
  3.3 0.8 %copy-start.4 = (bf16[128,118]{0,1:T(8,128)(2,1)S(1)}, bf16[128,118]{0,1:T(8,128)(2,1)}, u32[]{:S(2)}) copy-start(bf16[128,118]{0,1:T(8,128)(2,1)} %param.10) | copy-start | bytes 90628
  3.4 1.0 %copy-start.1 = (bf16[1,1152,128]{2,1,0:T(8,128)(2,1)S(1)}, bf16[1,1152,128]{2,1,0:T(8,128)(2,1)}, u32[]{:S(2)}) copy-start(bf16[1,1152,128]{2,1,0:T(8,128)(2,1)} %param.9) | copy-start | bytes 884740

commit v3 on v2

--- a/solution.py
+++ b/solution.py
@@ -266,14 +266,49 @@
         remote(w_ref.at[own_half], wall_ref.at[ph, own_half], w_send.at[k], w_recv.at[k], phase_peer(k))
         for k in range(1, phases)
     ]
-    row_copies = [
-        remote(cam_ref.at[ph], x_ref.at[own_rows], row_send.at[k], row_recv.at[k], tile_peer(k))
-        for k in range(1, tiles)
-    ]
-    code_copies = [
-        remote(code_ref, codes_ref.at[:, own_lanes], code_send.at[k], code_recv.at[k], tile_peer(k))
-        for k in range(1, tiles)
-    ]
+    cams = pos // width
+
+    def piece(row, c):
+        return pl.ds(pl.multiple_of(row * pos + c * width, 16), width)
+
+    def hop(row, c, step):
+        return pltpu.make_async_remote_copy(
+            src_ref=x_ref.at[piece(row, c)], dst_ref=x_ref.at[piece(row, c)],
+            send_sem=row_send.at[(step + 1) // 2, row, c], recv_sem=row_recv.at[row, c],
+            device_id=(ph, ti + step, dp), device_id_type=MESH,
+        )
+
+    def own_hop(c, step):
+        return pltpu.make_async_remote_copy(
+            src_ref=cam_ref.at[ph, c * width : (c + 1) * width], dst_ref=x_ref.at[piece(ti, c)],
+            send_sem=row_send.at[(step + 1) // 2, ti, c], recv_sem=row_recv.at[ti, c],
+            device_id=(ph, ti + step, dp), device_id_type=MESH,
+        )
+
+    def relay(act_own, act):
+        for c in range(cams):
+            for step in (1, -1):
+                if act_own is not None:
+                    @pl.when((ti + step >= 0) & (ti + step < tiles))
+                    def _():
+                        act_own(own_hop(c, step))
+        for d in act:
+            for c in range(cams):
+                for step in (1, -1):
+                    source = ti - step * d
+                    @pl.when((source >= 0) & (source < tiles))
+                    def _():
+                        if act_own is None:
+                            hop(source, c, -step).wait_recv()
+
+                        @pl.when((ti + step >= 0) & (ti + step < tiles))
+                        def _():
+                            if act_own is None:
+                                hop(source, c, step).start()
+                            else:
+                                hop(source, c, step).wait_send()
+
+    relay(lambda copy: copy.start(), ())
     own = [
         pltpu.make_async_copy(cam_ref.at[ph], x_ref.at[own_rows], local_sem.at[0]),
         pltpu.make_async_copy(code_ref, codes_ref.at[:, own_lanes], local_sem.at[1]),
@@ -281,6 +316,7 @@
     ]
     for copy in own:
         copy.start()
+    relay(None, (1,))
 
     edge = jnp.zeros((pos, cols3), BF16)
     z_ref[pl.ds(0, pos), :] = edge
@@ -289,6 +325,7 @@
     acc_w[...] = jnp.zeros_like(acc_w)
 
     up_ref[...] = cot_ref[...].astype(F32).T.astype(BF16)
+    relay(None, range(2, tiles - 1))
     forwards = []
     for k in range(1, phases):
         w_copies[k - 1].wait_recv()
@@ -297,21 +334,27 @@
             remote(wall_ref.at[source, own_half], wall_ref.at[source, own_half],
                    f_send.at[k], f_recv.at[k], partner)
         )
-    for copy in own + row_copies + code_copies + forwards:
+    relay(None, (tiles - 1,))
+    for copy in own + forwards:
         copy.wait()
+    relay(lambda copy: copy.wait_send(), range(1, tiles))
+    code_copies = [
+        remote(code_ref, codes_ref.at[:, own_lanes], code_send.at[k], code_recv.at[k], tile_peer(k))
+        for k in range(1, tiles)
+    ]
     for copy in w_copies:
         copy.wait_send()
 
     @pl.loop(0, phases)
     def _(s):
-        @pl.loop(0, tiles, unroll=2)
+        @pl.loop(0, tiles, unroll=4)
         def _(u):
             rows = x_ref[pl.ds(pl.multiple_of(u * pos, 16), pos), :]
             at = pl.ds(pl.multiple_of((u + 1) * pos, 16), pos)
             for e, part in enumerate(with_side_columns(rows, width)):
                 z_ref[at, e * channels : (e + 1) * channels] = part
 
-        @pl.loop(0, tiles, unroll=2)
+        @pl.loop(0, tiles, unroll=4)
         def _(u):
             at = pl.ds(pl.multiple_of(u * pos, 16), pos)
             patches = jnp.concatenate(
@@ -355,6 +398,9 @@
         1.0, 0.0,
     ).astype(BF16)
     window = grid_rows + 2
+
+    for copy in code_copies:
+        copy.wait()
 
     def add_blocks(u):
         back_ref[...] = wt_ref[u].astype(F32).T.astype(BF16)
@@ -499,7 +545,7 @@
         pltpu.VMEM((16, cols), F32),
         pltpu.VMEM((16, cols), F32),
         dma((3,)),
-        dma((tiles,)), dma((tiles,)), dma((tiles,)), dma((tiles,)),
+        dma((2, tiles, cams)), dma((tiles, cams)), dma((tiles,)), dma((tiles,)),
         dma((phases,)), dma((phases,)), dma((phases,)), dma((phases,)),
         dma((tiles,)), dma((tiles,)),
         dma(()), dma(()),

time: 63.9 us -> 56.5 us (0.88)
  Pallas kernels: 57.9 us -> 50.5 us
    pallas_call x1, Pallas kernels: 57.9 us -> 50.5 us  [fused_body(): pl.pallas_call(functools.partial(fused_kernel, dims), out_shape=(jax.Shap...]
where the time goes in v3:
time: 56.5 us; the launch traced here: 56.3 us
  Pallas kernels  50.5 us (89%)
  local copies, waits for them, and re-layouts  4.96 us (9%)
  between operations  0.82 us (1%)
    pallas_call x1, Pallas kernels, fused_body(): pl.pallas_call(functools.partial(fused_kernel, dims), out_shape=(jax.Shap...  50.5 us
    unnamed x19, local copies, waits for them, and re-layouts  2.97 us
    reshape x1, local copies, waits for them, and re-layouts, fused_body(): point_slot.reshape(groups, NSEG, BLK, seg).transpose(0, 2, 1, 3)  1.24 us

profile of v3, /device:TPU:0, one launch (start us, length us, event | category | flops | bytes accessed | tf_op | source)
XLA Modules:
  0.0 56.3 jit_solution(8383344347480573325)
XLA Ops:
  0.6 1.2 %reshape.79 = s32[132,2,4,59]{3,2,1,0:T(4,128)S(1)} reshape(s32[1,1,264,236]{3,2,1,0:T(8,128)} %param.12) | data formatting | bytes 498432 | tf_op jit(solution)/shard_map/reshape | solution.py:514
  1.9 0.1 copy.16
  2.0 0.3 copy.20
  2.3 0.2 pad.9.clone
  2.5 0.0 copy-start.6
  2.5 0.0 copy-start.5
  2.5 0.0 copy-start.2
  2.5 0.0 copy-start.3
  2.6 0.0 copy-start
  2.6 0.6 %copy-done.6 = s32[1,1,264,1]{2,3,1,0:T(1,128)S(1)} copy-done((s32[1,1,264,1]{2,3,1,0:T(1,128)S(1)}, s32[1,1,264,1]{2,3,1,0:T(1,128)}, u32[]{:S(2)}) %copy-start.6) | copy-done | bytes 1080
  3.2 0.1 add.21
  3.3 0.0 copy-start.4
  3.3 0.1 add.22
  3.4 0.0 copy-done.5
  3.4 0.0 copy-start.1
  3.4 0.1 copy.18
  3.5 0.1 reshape.82
  3.7 0.3 copy-done.4
  4.1 0.1 copy.19.dw_ref
  4.2 0.0 copy-done.2
  4.2 0.0 copy-done.3
  4.2 0.0 copy-done
  4.2 0.2 copy-done.1
  4.5 50.5 %lift_splat.1 = (bf16[1024,128]{1,0:T(8,128)(2,1)S(1)}, f32[2,16,1152]{2,1,0:T(8,128)S(1)}) custom-call(bf16[4,528,128]{2,1,0:T(8,128)(2,1)S(1)} %bitcast.19, bf16[1152,128]{1,0:T(8,128)(2,1)S(1)} %bitcast.20, bf16[128,256]{1,0:T(8,128)(2,1)S(1)} %copy.19.dw_ref, s32[528,256]{1,0:T(8,128)S(1)} %bitcast.18, s32[1,4224]{1,0:T(1,128)S(1)} %compare_select_fusion.code_ref, ...), custom_call_target="tpu_custom_call" | custom-call | tf_op jit(solution)/shard_map/lift_splat/pallas_call | solution.py:556
  55.0 0.7 %copy.26 = bf16[1,1,4,256,128]{4,3,2,1,0:T(8,128)(2,1)} copy(bf16[1,1,4,256,128]{4,3,2,1,0:T(8,128)(2,1)S(1)} %bitcast.22) | data formatting | bytes 524288
  55.7 0.7 %copy.27 = f32[32,1152]{1,0:T(8,128)} copy(f32[32,1152]{1,0:T(8,128)S(1)} %bitcast.23) | data formatting | bytes 294912
  (5 shorter events, 0.1 us)
Async XLA Ops:
  2.5 0.7 %copy-start.6 = (s32[1,1,264,1]{2,3,1,0:T(1,128)S(1)}, s32[1,1,264,1]{2,3,1,0:T(1,128)}, u32[]{:S(2)}) copy-start(s32[1,1,264,1]{2,3,1,0:T(1,128)} %param.11) | copy-start | bytes 3172
  2.5 0.9 %copy-start.5 = (s32[1,1,264,16]{2,3,1,0:T(8,128)S(1)}, s32[1,1,264,16]{2,3,1,0:T(8,128)}, u32[]{:S(2)}) copy-start(s32[1,1,264,16]{2,3,1,0:T(8,128)} %param.13) | copy-start | bytes 50692
  2.5 1.7 %copy-start.2 = (bf16[1152,128]{1,0:T(8,128)(2,1)S(1)}, bf16[1152,128]{1,0:T(8,128)(2,1)}, u32[]{:S(2)}) copy-start(bf16[1152,128]{1,0:T(8,128)(2,1)} %bw_ref.1) | copy-start | bytes 884740
  2.5 1.7 %copy-start.3 = (bf16[1,1,4,256,128]{4,3,2,1,0:T(8,128)(2,1)S(1)}, bf16[1,1,4,256,128]{4,3,2,1,0:T(8,128)(2,1)}, u32[]{:S(2)}) copy-start(bf16[1,1,4,256,128]{4,3,2,1,0:T(8,128)(2,1)} %param.15) | copy-start | bytes 786436
  2.6 1.6 %copy-start = (bf16[4,1,3,1,176,128]{5,4,3,2,1,0:T(8,128)(2,1)S(1)}, bf16[4,1,3,1,176,128]{5,4,3,2,1,0:T(8,128)(2,1)}, u32[]{:S(2)}) copy-start(bf16[4,1,3,1,176,128]{5,4,3,2,1,0:T(8,128)(2,1)} %param.8) | copy-start | bytes 1622020
  3.3 0.8 %copy-start.4 = (bf16[128,118]{0,1:T(8,128)(2,1)S(1)}, bf16[128,118]{0,1:T(8,128)(2,1)}, u32[]{:S(2)}) copy-start(bf16[128,118]{0,1:T(8,128)(2,1)} %param.10) | copy-start | bytes 90628
  3.4 1.0 %copy-start.1 = (bf16[1,1152,128]{2,1,0:T(8,128)(2,1)S(1)}, bf16[1,1152,128]{2,1,0:T(8,128)(2,1)}, u32[]{:S(2)}) copy-start(bf16[1,1152,128]{2,1,0:T(8,128)(2,1)} %param.9) | copy-start | bytes 884740
